TPU v7x, 256 devices: a whole 4x4x8 slice. The times are simulated.
256 devices in a mesh: tm: 8 (over y, core), pencil: 32 (over z, x).
Axes of the slice: x: 4, y: 4, z: 8, core: 2. Of those that a mesh axis runs over, the one named last changes fastest.
Arguments:
- initial: float32 [128, 64, 128], P('pencil'), may hold values from -6 to 6
- conductivity: float32 [128, 64, 128], P('pencil'), may hold values from 0.25 to 4
- source: float32 [128, 64, 128], P('pencil'), may hold values from -2 to 2.7
Outputs:
- final_states: float32 [8, 128, 64, 128], P('tm', 'pencil')
All inputs are finite; a program needn't handle non-finite values.
Results may differ from a plain program's by a relative error of at most 0.0002.
Values sent between devices are 32-bit elements; how exact they have to be, the bound alone decides.
A program may use at most 256 MiB of HBM per device.

v0:
```python
import jax
import jax.numpy as jnp
from jax import lax
from jax.experimental import pallas as pl
from jax.experimental.pallas import tpu as pltpu
from jax.sharding import PartitionSpec as P

MESH = pl.DeviceIdType.MESH
FINE = 4
ITERS = 2
SLICES = 8
NA = 8
NB = 4
BZ = 16
BY = 16
SLAB = 4
NX = 128
NY = 64
STEPS = ITERS * FINE
fine_dt = 0.5
coarse_dt = 2.0
vertical_ratio = 64.0


def harmonic(one, other):
    return 2.0 * one * other / (one + other)


def shift(values, amount, axis):
    return pltpu.roll(values, amount % values.shape[axis], axis)


def masked_faces(kappa, factor, axis):
    size = kappa.shape[axis]
    where = lax.broadcasted_iota(jnp.int32, kappa.shape, axis)
    faces = factor * harmonic(kappa, shift(kappa, -1, axis))
    return jnp.where(where == size - 1, 0.0, faces)


def cyclic_setup(faces, axis, store):
    size = faces.shape[axis]
    below = shift(faces, 1, axis)
    main = 1.0 + faces + below
    low, high = -below, -faces
    level, stride = 0, 1
    while stride < size:
        inverse = 1.0 / main
        alpha = -low * shift(inverse, stride, axis)
        beta = -high * shift(inverse, -stride, axis)
        store(level, alpha, beta)
        main = main + alpha * low + beta * high
        low, high = (alpha * shift(low, stride, axis), beta * shift(high, -stride, axis))
        level, stride = level + 1, stride * 2
    store(None, 1.0 / main, None)


def cyclic_apply(values, axis, alpha, beta, inverse):
    size = values.shape[axis]
    level, stride = 0, 1
    while stride < size:
        values = (
            values
            + alpha(level) * shift(values, stride, axis)
            + beta(level) * shift(values, -stride, axis)
        )
        level, stride = level + 1, stride * 2
    return values * inverse


def tree_sum(terms):
    terms = list(terms)
    while len(terms) > 1:
        terms = [
            terms[i] + terms[i + 1] if i + 1 < len(terms) else terms[i]
            for i in range(0, len(terms), 2)
        ]
    return terms[0]


def kernel(
    init_ref, kap_ref, src_ref, out_ref,
    Kb, Sb, Kz, Gz, Gy, tz_s, tz_r, ty_s, ty_r,
    Ew, Lw, Uw, Mw, Cz, Cy, Wz, Wy, Xc, CXc, CYc,
    V, Fs, ST, FB, UB, mz_s, mz_r, my_s, my_r,
    r0, s0, r1, s1, rz, szm, ry, sym, rF, sF, rS, sS, rO, sO,
):
    t = lax.axis_index("tm")
    p = lax.axis_index("pencil")
    a = lax.div(p, 4)
    b = lax.rem(p, 4)
    layer_own = lax.div(t, 2)
    is_owner = lax.rem(t, 2) == 0

    def at_z(da, bb):
        return (t, 4 * lax.rem(a + da, NA) + bb)

    def send(src, dst, ssem, rsem, dev):
        pltpu.make_async_remote_copy(
            src_ref=src, dst_ref=dst, send_sem=ssem, recv_sem=rsem,
            device_id=dev, device_id_type=MESH,
        ).start()

    def wait_bytes(ref, sem):
        pltpu.make_async_copy(ref, ref, sem).wait()

    barrier = pltpu.get_barrier_semaphore()

    def greet_plane(i, c):
        g = lax.rem(t * NB + b + i, SLICES * NB)
        pl.semaphore_signal(
            barrier, inc=1, device_id=(lax.div(g, NB), 4 * a + lax.rem(g, NB)), device_id_type=MESH
        )
        return c

    def greet_ring(i, c):
        pl.semaphore_signal(barrier, inc=1, device_id=at_z(i, b), device_id_type=MESH)
        return c

    def greet_side(i, c):
        other = lax.rem(b + i, NB)
        pl.semaphore_signal(barrier, inc=1, device_id=at_z(1, other), device_id_type=MESH)
        pl.semaphore_signal(barrier, inc=1, device_id=at_z(NA - 1, other), device_id_type=MESH)
        return c

    lax.fori_loop(1, SLICES * NB, greet_plane, 0)
    lax.fori_loop(1, NA, greet_ring, 0)
    lax.fori_loop(1, NB, greet_side, 0)
    pl.semaphore_wait(barrier, (SLICES * NB - 1) + (NA - 1) + 2 * (NB - 1))

    def window(bb):
        return pl.multiple_of(jnp.minimum(jnp.maximum(16 * bb - 8, 0), 32), 8)

    mine = pl.ds(4 * b, SLAB)
    for i in range(1, NB):
        other = lax.rem(b + i, NB)
        send(kap_ref.at[:, pl.ds(window(other), 32), :], Kb.at[mine], s0.at[0], r0.at[0], at_z(0, other))
    for side, layer, da in ((3, SLAB - 1, 1), (0, 0, NA - 1)):

        @pl.when(b == side)
        def _():
            for other in range(NB):
                send(
                    kap_ref.at[layer, pl.ds(16 * other, 16), :],
                    Kz.at[0 if side == 3 else 1],
                    s0.at[2], r0.at[2 if side == 3 else 3], at_z(da, other),
                )

    for i in range(1, NB):
        other = lax.rem(b + i, NB)
        send(
            src_ref.at[:, pl.ds(pl.multiple_of(16 * other, 16), 16), :],
            Sb.at[mine], s0.at[1], r0.at[1], at_z(0, other),
        )
    pltpu.make_async_copy(kap_ref.at[:, pl.ds(window(b), 32), :], Kb.at[mine], r0.at[0]).start()
    pltpu.make_async_copy(
        src_ref.at[:, pl.ds(pl.multiple_of(16 * b, 16), 16), :], Sb.at[mine], r0.at[1]
    ).start()

    @pl.when(is_owner)
    def _():
        kappa = kap_ref[layer_own]

        def keep_x(level, one, other):
            if level is None:
                CXc[14] = one
            else:
                CXc[2 * level] = one
                CXc[2 * level + 1] = other

        def keep_y(level, one, other):
            if level is None:
                CYc[12] = one
            else:
                CYc[2 * level] = one
                CYc[2 * level + 1] = other

        cyclic_setup(masked_faces(kappa, coarse_dt, 1), 1, keep_x)
        cyclic_setup(masked_faces(kappa, coarse_dt, 0), 0, keep_y)

    def coarse(values):
        values = cyclic_apply(values, 1, lambda l: CXc[2 * l], lambda l: CXc[2 * l + 1], CXc[14])
        return cyclic_apply(values, 0, lambda l: CYc[2 * l], lambda l: CYc[2 * l + 1], CYc[12])

    wait_bytes(Kb, r0.at[0])
    wait_bytes(Kz.at[0], r0.at[2])
    wait_bytes(Kz.at[1], r0.at[3])
    row0 = 16 * b - window(b)

    def kappa_z(z):
        return Kb[pl.ds(pl.multiple_of(z * 32 + row0, 8), 16), :]

    def kappa_y(y):
        return Kb2[pl.ds(jnp.minimum(jnp.maximum(row0 + y, 0), 31), 16, stride=32), :]

    Kb2 = Kb.reshape(BZ * 32, NX)
    kappa_z = lambda z: Kb2[pl.ds(pl.multiple_of(z * 32 + row0, 8), 16), :]

    def two_port(G, ts, first, inner, last, lowest, highest, factor, length):
        previous = first
        for i in range(length + 1):
            following = inner(i) if i < length else last
            face = factor * harmonic(previous, following)
            if i == 0:
                face = jnp.where(lowest, 0.0, face)
            if i == length:
                face = jnp.where(highest, 0.0, face)
            G[i] = face
            previous = following
        link = G[0]
        ground_low = jnp.zeros_like(link)
        ground_high = jnp.ones_like(link)
        for i in range(1, length):
            face = G[i]
            part = 1.0 / (link + ground_high + face)
            ground_low = ground_low + link * ground_high * part
            ground_high_new = 1.0 + face * ground_high * part
            link = link * face * part
            ground_high = ground_high_new
        ts[0] = ground_low
        ts[1] = link
        ts[2] = ground_high

    two_port(Gz, tz_s, Kz[0], kappa_z, Kz[1], a == 0, a == NA - 1, fine_dt * vertical_ratio, BZ)
    for i in range(1, NA):
        send(tz_s, tz_r.at[a], s1.at[0], r1.at[0], at_z(i, b))
    two_port(Gy, ty_s, kappa_y(-1), kappa_y, kappa_y(BY), b == 0, b == NB - 1, fine_dt, BY)
    for i in range(1, NB):
        send(ty_s, ty_r.at[b], s1.at[1], r1.at[1], at_z(0, lax.rem(b + i, NB)))
    pltpu.make_async_copy(tz_s, tz_r.at[a], r1.at[0]).start()
    pltpu.make_async_copy(ty_s, ty_r.at[b], r1.at[1]).start()

    def give(it, n):
        for other in range(NB):
            src = UB.at[it, n, pl.ds(16 * other, 16), :]
            dst = ST.at[BZ * it + 4 * b + layer_own]
            own = jnp.logical_and(n == t, other == b)

            @pl.when(own)
            def _():
                pltpu.make_async_copy(src, dst, rS.at[it]).start()

            @pl.when(jnp.logical_not(own))
            def _():
                send(src, dst, sS.at[it], rS.at[it], (n, 4 * a + other))

    @pl.when(is_owner)
    def _():
        heat = coarse_dt * src_ref[layer_own]
        UB[0, 0] = init_ref[layer_own]
        UB[1, 0] = init_ref[layer_own]
        give(0, 0)

        def advance(n, c):
            UB[0, n] = coarse(UB[0, n - 1] + heat)
            give(0, n)
            return c

        lax.fori_loop(1, SLICES, advance, 0)
        UB[0, SLICES] = coarse(UB[0, SLICES - 1] + heat)

    for z in range(BZ):
        kappa = kappa_z(z)

        def keep(level, one, other, z=z):
            if level is None:
                Xc[14, 16 * z : 16 * z + 16] = one
            else:
                Xc[2 * level, 16 * z : 16 * z + 16] = one
                Xc[2 * level + 1, 16 * z : 16 * z + 16] = other

        cyclic_setup(masked_faces(kappa, fine_dt, 1), 1, keep)

    def split_setup(G, tr, C, W, place, count, length):
        down = jnp.ones_like(G[0])
        Ew[0] = down
        for j in range(count):
            ground_low, link, ground_high = tr[j, 0], tr[j, 1], tr[j, 2]
            passed = link / (link + ground_low + down)
            Mw[j] = passed
            down = ground_high + passed * (ground_low + down)
            Ew[j + 1] = down
        up = jnp.zeros_like(down)
        for j in range(count - 1, -1, -1):
            ground_low, link, ground_high = tr[j, 0], tr[j, 1], tr[j, 2]
            Uw[j] = up
            passed = link / (link + ground_high + up)
            Lw[j] = passed
            up = ground_low + passed * (ground_high + up)
        one = jnp.ones_like(down)
        below, above = [None], [None]
        w = jnp.where(place >= 1, one, 0.0)
        below.append(w)
        for i in range(2, count):
            w = w * Lw[lax.rem(place + count - i + 1, count)]
            below.append(jnp.where(place >= i, w, 0.0))
        w = one
        above.append(jnp.where(place + 1 < count, w, 0.0))
        for i in range(2, count):
            w = w * Mw[lax.rem(place + i - 1, count)]
            above.append(jnp.where(place + i < count, w, 0.0))
        for i in range(1, count):
            W[i - 1] = below[count - i]
            W[count - 1 + i - 1] = above[i]
        under = Ew[place]
        over = Uw[place]
        floor = G[0]
        seen = 1.0 + floor * under / (floor + under)
        last = length - 1
        for i in range(length - 1):
            face = G[i + 1]
            inverse = 1.0 / (face + seen)
            C[1, i] = inverse
            C[0, i] = face * inverse
            seen = 1.0 + face * seen * inverse
        C[1, last] = 1.0 / (seen + over)
        part = one
        C[3, last] = part
        for i in range(length - 2, -1, -1):
            part = part * C[0, i]
            C[3, i] = part
        seen = 1.0 + over
        steps = [None] * length
        for i in range(length - 2, -1, -1):
            face = G[i + 1]
            inverse = 1.0 / (face + seen)
            steps[i + 1] = face * inverse
            seen = 1.0 + face * seen * inverse
        part = floor / (floor + seen)
        C[2, 0] = part
        for i in range(1, length):
            part = part * steps[i]
            C[2, i] = part
        C[0, last] = (floor + seen) / (seen * (floor + under) + floor * under)

    wait_bytes(tz_r, r1.at[0])
    split_setup(Gz, tz_r, Cz, Wz, a, NA, BZ)
    wait_bytes(ty_r, r1.at[1])
    split_setup(Gy, ty_r, Cy, Wy, b, NB, BY)
    wait_bytes(Sb, r0.at[1])

    def split_apply(load, store, C, W, ms, mr, ssem, rsem, st, place, count, length, device):
        rows = [load(i) for i in range(length)]
        last = length - 1
        ms[st, 0] = C[1, last] * tree_sum(C[3, i] * rows[i] for i in range(length))
        ms[st, 1] = C[0, last] * tree_sum(C[2, i] * rows[i] for i in range(length))
        for i in range(1, count):
            which = jnp.where(place + i < count, 0, 1)
            send(ms.at[st, which], mr.at[st, count - 1 - i], ssem.at[st], rsem.at[st], device(i))
        swept = [rows[0]]
        for i in range(1, length):
            swept.append(rows[i] + C[0, i - 1] * swept[i - 1])
        solved = [None] * length
        solved[last] = C[1, last] * swept[last]
        for i in range(length - 2, -1, -1):
            solved[i] = C[1, i] * swept[i] + C[0, i] * solved[i + 1]
        wait_bytes(mr.at[st], rsem.at[st])
        got = [mr[st, i] for i in range(count - 1)]
        low = tree_sum(W[i] * got[i] for i in range(count - 1))
        high = tree_sum(W[count - 1 + i] * got[i] for i in range(count - 1))
        for i in range(length):
            store(i, solved[i] + C[2, i] * low + C[3, i] * high)

    def fine_step(it, s):
        st = it * FINE + s
        for z in range(0, BZ, 2):
            rows = pl.ds(16 * z, 32)
            start = V[rows] + fine_dt * Sb[z : z + 2].reshape(32, NX)
            V[rows] = cyclic_apply(
                start, 1, lambda l: Xc[2 * l, rows], lambda l: Xc[2 * l + 1, rows], Xc[14, rows]
            )

        def store_y(y, value):
            V[pl.ds(y, BZ, stride=BY), :] = value

        split_apply(
            lambda y: V[pl.ds(y, BZ, stride=BY), :], store_y,
            Cy, Wy, my_s, my_r, sym, ry, st, b, NB, BY, lambda i: at_z(0, lax.rem(b + i, NB)),
        )

        def store_z(z, value):
            V[pl.ds(16 * z, 16), :] = value

        split_apply(
            lambda z: V[pl.ds(16 * z, 16), :], store_z,
            Cz, Wz, mz_s, mz_r, szm, rz, st, a, NA, BZ, lambda i: at_z(i, b),
        )

    for it in range(ITERS):
        wait_bytes(ST.at[pl.ds(BZ * it, BZ)], rS.at[it])
        for z in range(BZ):
            V[pl.ds(16 * z, 16), :] = ST[BZ * it + z]

        def one_step(s, c):
            fine_step(it, s)
            return c

        lax.fori_loop(0, FINE, one_step, 0)
        for z in range(BZ):
            Fs[it, z] = V[pl.ds(16 * z, 16), :]

        def hand_in(l, c):
            other = lax.div(l, 4)
            target = 2 * lax.rem(l, 4)
            dst = FB.at[it, t, pl.ds(pl.multiple_of(16 * b, 16), 16), :]
            own = jnp.logical_and(target == t, other == b)

            @pl.when(own)
            def _():
                pltpu.make_async_copy(Fs.at[it, l], dst, rF.at[it, t]).start()

            @pl.when(jnp.logical_not(own))
            def _():
                send(Fs.at[it, l], dst, sF.at[it], rF.at[it, t], (target, 4 * a + other))

            return c

        lax.fori_loop(0, BZ, hand_in, 0)

        @pl.when(is_owner)
        def _():
            last_turn = it == ITERS - 1

            def finish(n, value):
                UB[it + 1, n + 1] = UB[it, n + 1] + value
                if last_turn:
                    src = UB.at[it + 1, n + 1]
                    dst = out_ref.at[0, layer_own]

                    @pl.when(n == t)
                    def _():
                        pltpu.make_async_copy(src, dst, rO).start()

                    @pl.when(n != t)
                    def _():
                        send(src, dst, sO, rO, (n, p))

            def correct(n, before):
                wait_bytes(FB.at[it, n], rF.at[it, n])
                value = coarse(before) + (FB[it, n] - UB[it, n + 1])
                finish(n, value)
                if not last_turn:
                    @pl.when(n + 1 < SLICES)
                    def _():
                        give(it + 1, n + 1)
                return value

            if not last_turn:
                give(it + 1, 0)
            lax.fori_loop(0, SLICES, correct, jnp.zeros((NY, NX), jnp.float32))

    wait_bytes(out_ref, rO)
    wait_bytes(Kb.at[pl.ds(0, 12)], s0.at[0])
    wait_bytes(Sb.at[pl.ds(0, 12)], s0.at[1])

    @pl.when(jnp.logical_or(b == 0, b == NB - 1))
    def _():
        wait_bytes(ST.at[pl.ds(0, NB)], s0.at[2])

    wait_bytes(tz_r.at[pl.ds(0, NA - 1)], s1.at[0])
    wait_bytes(ty_r.at[pl.ds(0, NB - 1)], s1.at[1])

    def drain(st, c):
        wait_bytes(mz_r.at[st], szm.at[st])
        wait_bytes(my_r.at[st], sym.at[st])
        return c

    lax.fori_loop(0, STEPS, drain, 0)
    for it in range(ITERS):

        @pl.when(is_owner)
        def _():
            wait_bytes(Fs.at[it, pl.ds(0, BZ - 1)], sF.at[it])
            wait_bytes(ST.at[pl.ds(0, 31)], sS.at[it])

        @pl.when(jnp.logical_not(is_owner))
        def _():
            wait_bytes(Fs.at[it], sF.at[it])

    @pl.when(is_owner)
    def _():
        wait_bytes(FB.at[0, pl.ds(0, SLICES - 1)], sO)


def vm(*shape):
    return pltpu.VMEM(shape, jnp.float32)


def per_device(initial, conductivity, source):
    dma = pltpu.SemaphoreType.DMA
    line = (16, NX)
    return pl.pallas_call(
        kernel,
        out_shape=jax.ShapeDtypeStruct((1, SLAB, NY, NX), jnp.float32),
        in_specs=[pl.BlockSpec(memory_space=pltpu.VMEM)] * 3,
        out_specs=pl.BlockSpec(memory_space=pltpu.VMEM),
        scratch_shapes=[
            vm(BZ, 32, NX), vm(BZ, BY, NX), vm(2, *line), vm(BZ + 1, *line), vm(BY + 1, *line),
            vm(3, *line), vm(NA, 3, *line), vm(3, *line), vm(NB, 3, *line),
            vm(NA + 1, *line), vm(NA, *line), vm(NA, *line), vm(NA, *line),
            vm(4, BZ, *line), vm(4, BY, *line), vm(2 * (NA - 1), *line), vm(2 * (NB - 1), *line),
            vm(15, BZ * BY, NX), vm(15, NY, NX), vm(13, NY, NX),
            vm(BZ * BY, NX), vm(ITERS, BZ, *line), vm(ITERS * BZ, *line),
            vm(ITERS, SLICES, NY, NX), vm(ITERS + 1, SLICES + 1, NY, NX),
            vm(STEPS, 2, *line), vm(STEPS, NA - 1, *line), vm(STEPS, 2, *line), vm(STEPS, NB - 1, *line),
            dma((4,)), dma((3,)), dma((2,)), dma((2,)),
            dma((STEPS,)), dma((STEPS,)), dma((STEPS,)), dma((STEPS,)),
            dma((ITERS, SLICES)), dma((ITERS,)), dma((ITERS,)), dma((ITERS,)), dma, dma,
        ],
        compiler_params=pltpu.CompilerParams(
            collective_id=0, has_side_effects=True, vmem_limit_bytes=40 * 1024 * 1024
        ),
        name="parareal",
    )(initial, conductivity, source)


def solution(mesh):
    placed = P("pencil", None, None)
    return jax.shard_map(
        per_device,
        mesh=mesh,
        in_specs=(placed, placed, placed),
        out_specs=P("tm", "pencil", None, None),
        check_vma=False,
    )
```

profile of v0, /device:TPU:25, one launch (start us, length us, event | category | flops | bytes accessed | tf_op | source)
XLA Modules:
  0.0 122.7 jit_solution(16936788870334595782)
XLA Ops:
  0.0 0.0 copy-start
  0.0 0.9 copy-done
  0.9 0.0 copy-start.1
  0.9 0.9 copy-done.1
  1.8 0.0 copy-start.2
  1.8 0.9 copy-done.2
  2.7 119.3 %parareal.1 = f32[1,4,64,128]{3,2,1,0:T(8,128)S(1)} custom-call(f32[4,64,128]{2,1,0:T(8,128)S(1)} %copy-done, f32[4,64,128]{2,1,0:T(8,128)S(1)} %copy-done.1, f32[4,64,128]{2,1,0:T(8,128)S(1)} %copy-done.2), custom_call_target="tpu_custom_call" | custom-call | tf_op jit(solution)/shard_map/parareal/pallas_call | solution.py:491
  122.0 0.7 copy.5
Async XLA Ops:
  0.0 0.9 copy-start
  0.9 0.9 copy-start.1
  1.8 0.9 copy-start.2
where the time goes:
time: 123 us
  Pallas kernels  119 us (97%)
  local copies, waits for them, and re-layouts  3.37 us (3%)
    pallas_call x1, Pallas kernels, per_device(): pl.pallas_call(kernel, out_shape=jax.ShapeDtypeStruct((1, SLAB, NY, NX),...  119 us
    unnamed x7, local copies, waits for them, and re-layouts  3.37 us

commit v1 on v0

v1 whole, which is shorter than its diff:
```python
import jax
import jax.numpy as jnp
from jax import lax
from jax.experimental import pallas as pl
from jax.experimental.pallas import tpu as pltpu
from jax.sharding import PartitionSpec as P

MESH = pl.DeviceIdType.MESH
FINE = 4
ITERS = 2
SLICES = 8
NA = 8
NB = 4
NC = 2
BZ = 16
BY = 32
SLAB = 4
NX = 128
NY = 64
WIN = BY + 8
STEPS = ITERS * FINE
FAR_FIRST = (4, 3, 5, 2, 6, 1, 7)
fine_dt = 0.5
coarse_dt = 2.0
vertical_ratio = 64.0


def harmonic(one, other):
    return 2.0 * one * other / (one + other)


def tree_sum(terms):
    terms = list(terms)
    while len(terms) > 1:
        terms = [
            terms[i] + terms[i + 1] if i + 1 < len(terms) else terms[i]
            for i in range(0, len(terms), 2)
        ]
    return terms[0]


def turn(values, amount):
    grouped = values.reshape(-1, 8, NX)
    return pltpu.roll(grouped, amount % 8, 1).reshape(values.shape)


def block_ends(faces, length):
    link = faces[0]
    ground_low = jnp.zeros_like(link)
    ground_high = jnp.ones_like(link)
    for i in range(1, length):
        face = faces[i]
        part = 1.0 / (link + ground_high + face)
        ground_low = ground_low + link * ground_high * part
        ground_high, link = (1.0 + face * ground_high * part, link * face * part)
    return ground_low, link, ground_high


def block_coefficients(faces, under, over, length, C):
    floor = faces[0]
    seen = 1.0 + floor * under / (floor + under)
    last = length - 1
    for i in range(last):
        face = faces[i + 1]
        inverse = 1.0 / (face + seen)
        C[1, i] = inverse
        C[0, i] = face * inverse
        seen = 1.0 + face * seen * inverse
    C[1, last] = 1.0 / (seen + over)
    part = jnp.ones_like(floor)
    C[3, last] = part
    for i in range(last - 1, -1, -1):
        part = part * C[0, i]
        C[3, i] = part
    seen = 1.0 + over
    steps = [None] * length
    for i in range(last - 1, -1, -1):
        face = faces[i + 1]
        inverse = 1.0 / (face + seen)
        steps[i + 1] = face * inverse
        seen = 1.0 + face * seen * inverse
    part = floor / (floor + seen)
    C[2, 0] = part
    for i in range(1, length):
        part = part * steps[i]
        C[2, i] = part
    C[0, last] = (floor + seen) / (seen * (floor + under) + floor * under)


def block_edges(rows, C):
    last = len(rows) - 1
    return (
        C[1, last] * tree_sum(C[3, i] * row for i, row in enumerate(rows)),
        C[0, last] * tree_sum(C[2, i] * row for i, row in enumerate(rows)),
    )


def block_inner(rows, C):
    last = len(rows) - 1
    swept = [rows[0]]
    for i in range(1, last + 1):
        swept.append(rows[i] + C[0, i - 1] * swept[i - 1])
    solved = [None] * (last + 1)
    solved[last] = C[1, last] * swept[last]
    for i in range(last - 1, -1, -1):
        solved[i] = C[1, i] * swept[i] + C[0, i] * solved[i + 1]
    return solved


def local_setup(kappas, factor, C, W):
    length = len(kappas)
    position = lax.broadcasted_iota(jnp.int32, kappas[0].shape, 0) % 8
    faces = [None] + [
        factor * harmonic(kappas[i], kappas[i + 1]) for i in range(length - 1)
    ]
    top = factor * harmonic(kappas[length - 1], turn(kappas[0], -1))
    faces[0] = turn(jnp.where(position == 7, 0.0, top), 1)
    ground_low, link, ground_high = block_ends(faces, length)
    down = jnp.ones_like(link)
    for _ in range(8):
        under = turn(down, 1)
        down_part = link / (link + ground_low + under)
        down = ground_high + down_part * (ground_low + under)
    under = turn(down, 1)
    up = jnp.zeros_like(link)
    for _ in range(8):
        over = jnp.where(position == 7, 0.0, turn(up, -1))
        up_part = link / (link + ground_high + over)
        up = ground_low + up_part * (ground_high + over)
    over = jnp.where(position == 7, 0.0, turn(up, -1))
    low_part = link / (link + ground_high + over)
    high_part = link / (link + ground_low + under)
    below = jnp.ones_like(link)
    above = jnp.ones_like(link)
    for k in range(1, 8):
        if k > 1:
            below = below * turn(low_part, k - 1)
            above = above * turn(high_part, 1 - k)
        W[k - 1] = jnp.where(position >= k, below, 0.0)
        W[7 + k - 1] = jnp.where(position + k < 8, above, 0.0)
    block_coefficients(faces, under, over, length, C)


def local_apply(rows, C, W):
    up, down = block_edges(rows, C)
    low = tree_sum(W[k - 1] * turn(up, k) for k in range(1, 8))
    high = tree_sum(W[7 + k - 1] * turn(down, -k) for k in range(1, 8))
    solved = block_inner(rows, C)
    return [
        value + C[2, i] * low + C[3, i] * high for i, value in enumerate(solved)
    ]


def kernel(
    init_ref, kap_ref, src_ref, out_ref,
    Kb, Sb, Kz, Gz, Gy, tz_s, tz_r, ty_s, ty_r,
    Ez, Lz, Uz, Mz, Ey, Ly, Uy, My, Cz, Cy, Wz, Wy, Cx, Wx, T,
    Ki, Hi, CXc, WXc, CYc, WYc, Tc, Lc,
    ST, FB, UB, mz_s, mz_r, my_s, my_r,
    r0, s0, r1, s1, rz, szm, ry, sym, rF, sF, rS, sS, rO, sO, rI,
):
    t = lax.axis_index("tm")
    p = lax.axis_index("pencil")
    a = lax.div(p, NB)
    b = lax.rem(p, NB)
    y = lax.div(t, NC)
    half = lax.rem(t, NC)
    is_fine = lax.rem(b + y, 2) == 0
    is_owner = lax.rem(b + y, 2) == 1
    section = 2 * b + lax.div(y, 2)
    layer_own = 2 * lax.div(y, 2) + half

    def at_z(da):
        return (t, NB * lax.rem(a + da, NA) + b)

    def fine_device(n, h):
        bb = lax.div(n, 2)
        yy = lax.rem(bb, 2) + 2 * lax.rem(n, 2)
        return (NC * yy + h, NB * a + bb)

    def owner_device(bb, k):
        yy = lax.rem(bb + 1, 2) + 2 * lax.div(k, 2)
        return (NC * yy + lax.rem(k, 2), NB * a + bb)

    def send(src, dst, ssem, rsem, dev):
        pltpu.make_async_remote_copy(
            src_ref=src, dst_ref=dst, send_sem=ssem, recv_sem=rsem,
            device_id=dev, device_id_type=MESH,
        ).start()

    def wait_bytes(ref, sem):
        pltpu.make_async_copy(ref, ref, sem).wait()

    barrier = pltpu.get_barrier_semaphore()

    def greet_plane(i, c):
        g = lax.rem(t * NB + b + i, SLICES * NB)
        pl.semaphore_signal(
            barrier, inc=1, device_id=(lax.div(g, NB), NB * a + lax.rem(g, NB)), device_id_type=MESH
        )
        return c

    def greet_side(i, c):
        other = lax.rem(b + i, NB)
        for da in (1, NA - 1):
            pl.semaphore_signal(
                barrier, inc=1, device_id=(t, NB * lax.rem(a + da, NA) + other), device_id_type=MESH
            )
        return c

    for i in FAR_FIRST:
        pl.semaphore_signal(barrier, inc=1, device_id=at_z(i), device_id_type=MESH)
    lax.fori_loop(1, NB, greet_side, 0)
    lax.fori_loop(1, SLICES * NB, greet_plane, 0)

    @pl.when(is_owner)
    def _():
        pltpu.make_async_copy(kap_ref.at[layer_own], Ki.at[0], rI.at[0]).start()
        pltpu.make_async_copy(src_ref.at[layer_own], Ki.at[1], rI.at[1]).start()
        pltpu.make_async_copy(init_ref.at[layer_own], Ki.at[2], rI.at[2]).start()

    pl.semaphore_wait(barrier, (SLICES * NB - 1) + (NA - 1) + 2 * (NB - 1))

    first = pl.multiple_of(half * BY, 8)
    window = pl.ds(pl.multiple_of(half * (NY - WIN), 8), WIN)
    mine = pl.ds(SLAB * b, SLAB)
    even = lax.rem(y, 2)
    for i in range(2):
        target = even + 2 * i

        @pl.when(target != b)
        def _():
            send(kap_ref.at[:, window, :], Kb.at[mine], s0.at[0], r0.at[0], (t, NB * a + target))

        @pl.when(target == b)
        def _():
            pltpu.make_async_copy(kap_ref.at[:, window, :], Kb.at[mine], r0.at[0]).start()

    for side, layer, da in ((NB - 1, SLAB - 1, 1), (0, 0, NA - 1)):

        @pl.when(b == side)
        def _():
            for i in range(2):
                send(
                    kap_ref.at[layer, pl.ds(first, BY), :],
                    Kz.at[0 if da == 1 else 1],
                    s0.at[2], r0.at[2 if da == 1 else 3],
                    (t, NB * lax.rem(a + da, NA) + even + 2 * i),
                )

    for i in range(2):
        target = even + 2 * i

        @pl.when(target != b)
        def _():
            send(src_ref.at[:, pl.ds(first, BY), :], Sb.at[mine], s0.at[1], r0.at[1], (t, NB * a + target))

        @pl.when(target == b)
        def _():
            pltpu.make_async_copy(src_ref.at[:, pl.ds(first, BY), :], Sb.at[mine], r0.at[1]).start()

    def give(it, n):
        for h in range(NC):
            send(
                UB.at[it, n, pl.ds(BY * h, BY), :],
                ST.at[it, pl.ds(pl.multiple_of(BY * (SLAB * b + layer_own), BY), BY), :],
                sS.at[it], rS.at[it], fine_device(n, h),
            )

    def coarse(values):
        Tc[:, 0:NY] = values.T
        rows = [Tc[pl.ds(i, 8, stride=16), :] for i in range(16)]
        for i, row in enumerate(local_apply(rows, CXc, WXc)):
            Tc[pl.ds(i, 8, stride=16), :] = row
        Lc[...] = Tc[:, 0:NY].T
        rows = [Lc[pl.ds(i, 8, stride=8), :] for i in range(8)]
        for i, row in enumerate(local_apply(rows, CYc, WYc)):
            Lc[pl.ds(i, 8, stride=8), :] = row
        return Lc[...]

    @pl.when(is_owner)
    def _():
        wait_bytes(Ki.at[0], rI.at[0])
        wait_bytes(Ki.at[1], rI.at[1])
        wait_bytes(Ki.at[2], rI.at[2])
        UB[0, 0] = Ki[2]
        UB[1, 0] = Ki[2]
        UB[2, 0] = Ki[2]
        give(0, 0)
        Tc[...] = jnp.ones_like(Tc)
        Tc[:, 0:NY] = Ki[0].T
        local_setup([Tc[pl.ds(i, 8, stride=16), :] for i in range(16)], coarse_dt, CXc, WXc)
        Lc[...] = Ki[0]
        local_setup([Lc[pl.ds(i, 8, stride=8), :] for i in range(8)], coarse_dt, CYc, WYc)
        heat = coarse_dt * Ki[1]
        Hi[...] = heat

        def advance(n, c):
            UB[0, n] = coarse(UB[0, n - 1] + Hi[...])
            give(0, n)
            return c

        lax.fori_loop(1, SLICES, advance, 0)
        UB[0, SLICES] = coarse(UB[0, SLICES - 1] + Hi[...])

    def split_setup(faces, tr, E, L, U, M, C, W, place, count, length):
        down = jnp.ones_like(faces[0])
        E[0] = down
        for j in range(count):
            ground_low, link, ground_high = tr[j, 0], tr[j, 1], tr[j, 2]
            passed = link / (link + ground_low + down)
            M[j] = passed
            down = ground_high + passed * (ground_low + down)
            E[j + 1] = down
        up = jnp.zeros_like(down)
        for j in range(count - 1, -1, -1):
            ground_low, link, ground_high = tr[j, 0], tr[j, 1], tr[j, 2]
            U[j] = up
            passed = link / (link + ground_high + up)
            L[j] = passed
            up = ground_low + passed * (ground_high + up)
        one = jnp.ones_like(down)
        below, above = [None], [None]
        part = one
        for i in range(1, count):
            if i > 1:
                part = part * L[lax.rem(place + count - i + 1, count)]
            below.append(jnp.where(place >= i, part, 0.0))
        part = one
        for i in range(1, count):
            if i > 1:
                part = part * M[lax.rem(place + i - 1, count)]
            above.append(jnp.where(place + i < count, part, 0.0))
        for i in range(1, count):
            W[i - 1] = below[count - i]
            W[count - 1 + i - 1] = above[i]
        block_coefficients(faces, E[place], U[place], length, C)

    def split_apply(load, store, C, W, ms, mr, ssem, rsem, st, place, count, length, order, device):
        rows = [load(i) for i in range(length)]
        up, down = block_edges(rows, C)
        ms[st, 0] = up
        ms[st, 1] = down
        for i in order:
            which = jnp.where(place + i < count, 0, 1)
            send(ms.at[st, which], mr.at[st, count - 1 - i], ssem.at[st], rsem.at[st], device(i))
        solved = block_inner(rows, C)
        wait_bytes(mr.at[st], rsem.at[st])
        got = [mr[st, i] for i in range(count - 1)]
        low = tree_sum(W[i] * got[i] for i in range(count - 1))
        high = tree_sum(W[count - 1 + i] * got[i] for i in range(count - 1))
        for i in range(length):
            store(i, solved[i] + C[2, i] * low + C[3, i] * high)

    @pl.when(is_fine)
    def _():
        wait_bytes(Kb, r0.at[0])
        wait_bytes(Kz.at[0], r0.at[2])
        wait_bytes(Kz.at[1], r0.at[3])
        row0 = 8 * half
        rows_of_k = Kb.reshape(BZ * WIN, NX)

        def kappa_z(z):
            return rows_of_k[pl.ds(pl.multiple_of(z * WIN + row0, 8), BY), :]

        def kappa_y(i):
            return rows_of_k[pl.ds(jnp.clip(row0 + i, 0, WIN - 1), BZ, stride=WIN), :]

        def outside(G, ts, first_k, inner, last_k, lowest, highest, factor, length):
            previous = first_k
            for i in range(length + 1):
                following = inner(i) if i < length else last_k
                face = factor * harmonic(previous, following)
                if i == 0:
                    face = jnp.where(lowest, 0.0, face)
                if i == length:
                    face = jnp.where(highest, 0.0, face)
                G[i] = face
                previous = following
            for i, part in enumerate(block_ends(G, length)):
                ts[i] = part

        outside(Gz, tz_s, Kz[0], kappa_z, Kz[1], a == 0, a == NA - 1, fine_dt * vertical_ratio, BZ)
        for i in FAR_FIRST:
            send(tz_s, tz_r.at[a], s1.at[0], r1.at[0], at_z(i))
        pltpu.make_async_copy(tz_s, tz_r.at[a], r1.at[0]).start()
        outside(Gy, ty_s, kappa_y(-1), kappa_y, kappa_y(BY), half == 0, half == 1, fine_dt, BY)
        partner = (t + 1 - 2 * half, p)
        send(ty_s, ty_r.at[half], s1.at[1], r1.at[1], partner)
        pltpu.make_async_copy(ty_s, ty_r.at[half], r1.at[1]).start()

        for z in range(BZ):
            T[pl.ds(BY * z, BY), :] = kappa_z(z)
        for tile in range(4):
            T[pl.ds(NX * tile, NX), :] = T[pl.ds(NX * tile, NX), :].T
        local_setup([T[pl.ds(i, 32, stride=16), :] for i in range(16)], fine_dt, Cx, Wx)

        wait_bytes(ty_r, r1.at[1])
        split_setup(Gy, ty_r, Ey, Ly, Uy, My, Cy, Wy, half, NC, BY)
        wait_bytes(tz_r, r1.at[0])
        split_setup(Gz, tz_r, Ez, Lz, Uz, Mz, Cz, Wz, a, NA, BZ)
        wait_bytes(Sb, r0.at[1])
        for z in range(BZ):
            Sb[z] = fine_dt * Sb[z]

        def fine_step(it, s):
            st = it * FINE + s
            V = ST.at[it]
            for tile in range(4):
                start = V[pl.ds(NX * tile, NX), :] + Sb[4 * tile : 4 * tile + 4].reshape(NX, NX)
                T[pl.ds(NX * tile, NX), :] = start.T
            rows = [T[pl.ds(i, 32, stride=16), :] for i in range(16)]
            for i, row in enumerate(local_apply(rows, Cx, Wx)):
                T[pl.ds(i, 32, stride=16), :] = row
            for tile in range(4):
                V[pl.ds(NX * tile, NX), :] = T[pl.ds(NX * tile, NX), :].T

            def store_y(i, value):
                V[pl.ds(i, BZ, stride=BY), :] = value

            split_apply(
                lambda i: V[pl.ds(i, BZ, stride=BY), :], store_y,
                Cy, Wy, my_s, my_r, sym, ry, st, half, NC, BY, (1,), lambda i: partner,
            )

            def store_z(i, value):
                V[pl.ds(BY * i, BY), :] = value

            split_apply(
                lambda i: V[pl.ds(BY * i, BY), :], store_z,
                Cz, Wz, mz_s, mz_r, szm, rz, st, a, NA, BZ, FAR_FIRST, at_z,
            )

        for it in range(ITERS):
            wait_bytes(ST.at[it], rS.at[it])

            def one_step(s, c):
                fine_step(it, s)
                return c

            lax.fori_loop(0, FINE, one_step, 0)

            def hand_in(i, c):
                bb = lax.rem(b + 2 + i, NB)
                for k in range(SLAB):
                    send(
                        ST.at[it, pl.ds(pl.multiple_of(BY * (SLAB * bb + k), BY), BY), :],
                        FB.at[it, section, pl.ds(first, BY), :],
                        sF.at[it], rF.at[it, section], owner_device(bb, k),
                    )
                return c

            lax.fori_loop(0, NB, hand_in, 0)

    @pl.when(is_owner)
    def _():
        for it in range(ITERS):
            last_turn = it == ITERS - 1

            def correct(n, before):
                wait_bytes(FB.at[it, n], rF.at[it, n])
                value = coarse(before) + (FB[it, n] - UB[it, n + 1])
                UB[it + 1, n + 1] = UB[it, n + 1] + value
                if last_turn:
                    src = UB.at[it + 1, n + 1]
                    dst = out_ref.at[0, layer_own]

                    @pl.when(n == t)
                    def _():
                        pltpu.make_async_copy(src, dst, rO).start()

                    @pl.when(n != t)
                    def _():
                        send(src, dst, sO, rO, (n, p))
                else:

                    @pl.when(n + 1 < SLICES)
                    def _():
                        give(it + 1, n + 1)
                return value

            if not last_turn:
                give(it + 1, 0)
            lax.fori_loop(0, SLICES, correct, jnp.zeros((NY, NX), jnp.float32))

    wait_bytes(out_ref, rO)

    @pl.when(is_fine)
    def _():
        wait_bytes(Kb.at[pl.ds(0, SLAB)], s0.at[0])
        wait_bytes(Sb.at[pl.ds(0, SLAB)], s0.at[1])
        wait_bytes(tz_r.at[pl.ds(0, NA - 1)], s1.at[0])
        wait_bytes(ty_s, s1.at[1])

        def drain(st, c):
            wait_bytes(mz_r.at[st], szm.at[st])
            wait_bytes(my_r.at[st], sym.at[st])
            return c

        lax.fori_loop(0, STEPS, drain, 0)
        for it in range(ITERS):
            wait_bytes(ST.at[it], sF.at[it])

    @pl.when(jnp.logical_or(b == 0, b == NB - 1))
    def _():
        wait_bytes(Kz, s0.at[2])

    @pl.when(is_owner)
    def _():
        wait_bytes(Kb.at[pl.ds(0, 2 * SLAB)], s0.at[0])
        wait_bytes(Sb.at[pl.ds(0, 2 * SLAB)], s0.at[1])
        for it in range(ITERS):
            wait_bytes(ST.at[it], sS.at[it])
        wait_bytes(FB.at[0, pl.ds(0, SLICES - 1)], sO)


def vm(*shape):
    return pltpu.VMEM(shape, jnp.float32)


def per_device(initial, conductivity, source):
    dma = pltpu.SemaphoreType.DMA
    zl = (BY, NX)
    yl = (BZ, NX)
    return pl.pallas_call(
        kernel,
        out_shape=jax.ShapeDtypeStruct((1, SLAB, NY, NX), jnp.float32),
        in_specs=[pl.BlockSpec(memory_space=pl.ANY)] * 3,
        out_specs=pl.BlockSpec(memory_space=pl.ANY),
        scratch_shapes=[
            vm(BZ, WIN, NX), vm(BZ, BY, NX), vm(2, *zl), vm(BZ + 1, *zl), vm(BY + 1, *yl),
            vm(3, *zl), vm(NA, 3, *zl), vm(3, *yl), vm(NC, 3, *yl),
            vm(NA + 1, *zl), vm(NA, *zl), vm(NA, *zl), vm(NA, *zl),
            vm(NC + 1, *yl), vm(NC, *yl), vm(NC, *yl), vm(NC, *yl),
            vm(4, BZ, *zl), vm(4, BY, *yl), vm(2 * (NA - 1), *zl), vm(2 * (NC - 1), *yl),
            vm(4, 16, 32, NX), vm(14, 32, NX), vm(BZ * BY, NX),
            vm(3, NY, NX), vm(NY, NX), vm(4, 16, 8, NX), vm(14, 8, NX),
            vm(4, 8, 8, NX), vm(14, 8, NX), vm(NX, NX), vm(NY, NX),
            vm(ITERS, BZ * BY, NX), vm(ITERS, SLICES, NY, NX), vm(ITERS + 1, SLICES + 1, NY, NX),
            vm(STEPS, 2, *zl), vm(STEPS, NA - 1, *zl), vm(STEPS, 2, *yl), vm(STEPS, NC - 1, *yl),
            dma((4,)), dma((3,)), dma((2,)), dma((2,)),
            dma((STEPS,)), dma((STEPS,)), dma((STEPS,)), dma((STEPS,)),
            dma((ITERS, SLICES)), dma((ITERS,)), dma((ITERS,)), dma((ITERS,)), dma, dma, dma((3,)),
        ],
        compiler_params=pltpu.CompilerParams(
            collective_id=0, has_side_effects=True, vmem_limit_bytes=48 * 1024 * 1024
        ),
        name="parareal",
    )(initial, conductivity, source)


def solution(mesh):
    placed = P("pencil", None, None)
    return jax.shard_map(
        per_device,
        mesh=mesh,
        in_specs=(placed, placed, placed),
        out_specs=P("tm", "pencil", None, None),
        check_vma=False,
    )
```

time: 123 us -> 113 us (0.919)
  Pallas kernels: 119 us -> 108 us
    pallas_call x1, Pallas kernels: 119 us -> 108 us  [per_device(): pl.pallas_call(kernel, out_shape=jax.ShapeDtypeStruct((1, SLAB, NY, NX),...]
where the time goes in v1:
time: 113 us; the launch traced here: 112 us
  Pallas kernels  108 us (96%)
  local copies, waits for them, and re-layouts  3.37 us (3%)
    pallas_call x1, Pallas kernels, per_device(): pl.pallas_call(kernel, out_shape=jax.ShapeDtypeStruct((1, SLAB, NY, NX),...  108 us
    unnamed x7, local copies, waits for them, and re-layouts  3.37 us

profile of v1, /device:TPU:25, one launch (start us, length us, event | category | flops | bytes accessed | tf_op | source)
XLA Modules:
  0.0 111.7 jit_solution(9376821933533388462)
XLA Ops:
  0.0 0.0 copy-start
  0.0 0.9 copy-done
  0.9 0.0 copy-start.1
  0.9 0.9 copy-done.1
  1.8 0.0 copy-start.2
  1.8 0.9 copy-done.2
  2.7 108.4 %parareal.1 = f32[1,4,64,128]{3,2,1,0:T(8,128)S(1)} custom-call(f32[4,64,128]{2,1,0:T(8,128)S(1)} %copy-done, f32[4,64,128]{2,1,0:T(8,128)S(1)} %copy-done.1, f32[4,64,128]{2,1,0:T(8,128)S(1)} %copy-done.2), custom_call_target="tpu_custom_call" | custom-call | tf_op jit(solution)/shard_map/parareal/pallas_call | solution.py:525
  111.1 0.7 copy.5
Async XLA Ops:
  0.0 0.9 copy-start
  0.9 0.9 copy-start.1
  1.8 0.9 copy-start.2

commit v2 on v1

--- a/solution.py
+++ b/solution.py
@@ -166,9 +166,12 @@
     y = lax.div(t, NC)
     half = lax.rem(t, NC)
     is_fine = lax.rem(b + y, 2) == 0
-    is_owner = lax.rem(b + y, 2) == 1
+    odd = lax.rem(b + y, 2) == 1
+    is_owner = jnp.logical_and(odd, half == 0)
+    is_helper = jnp.logical_and(odd, half == 1)
     section = 2 * b + lax.div(y, 2)
-    layer_own = 2 * lax.div(y, 2) + half
+    pair = lax.div(y, 2)
+    owned = pl.ds(2 * pair, 2)
 
     def at_z(da):
         return (t, NB * lax.rem(a + da, NA) + b)
@@ -179,8 +182,7 @@
         return (NC * yy + h, NB * a + bb)
 
     def owner_device(bb, k):
-        yy = lax.rem(bb + 1, 2) + 2 * lax.div(k, 2)
-        return (NC * yy + lax.rem(k, 2), NB * a + bb)
+        return (NC * (lax.rem(bb + 1, 2) + 2 * k), NB * a + bb)
 
     def send(src, dst, ssem, rsem, dev):
         pltpu.make_async_remote_copy(
@@ -193,33 +195,56 @@
 
     barrier = pltpu.get_barrier_semaphore()
 
-    def greet_plane(i, c):
-        g = lax.rem(t * NB + b + i, SLICES * NB)
-        pl.semaphore_signal(
-            barrier, inc=1, device_id=(lax.div(g, NB), NB * a + lax.rem(g, NB)), device_id_type=MESH
-        )
-        return c
-
-    def greet_side(i, c):
-        other = lax.rem(b + i, NB)
-        for da in (1, NA - 1):
-            pl.semaphore_signal(
-                barrier, inc=1, device_id=(t, NB * lax.rem(a + da, NA) + other), device_id_type=MESH
-            )
-        return c
-
-    for i in FAR_FIRST:
-        pl.semaphore_signal(barrier, inc=1, device_id=at_z(i), device_id_type=MESH)
-    lax.fori_loop(1, NB, greet_side, 0)
-    lax.fori_loop(1, SLICES * NB, greet_plane, 0)
+    def greet(dev):
+        pl.semaphore_signal(barrier, inc=1, device_id=dev, device_id_type=MESH)
+
+    on_side = jnp.logical_or(b == 0, b == NB - 1)
+
+    @pl.when(is_fine)
+    def _():
+        for i in FAR_FIRST:
+            greet(at_z(i))
+
+        @pl.when(b != NB - 1)
+        def _():
+            greet((t, NB * lax.rem(a + NA - 1, NA) + NB - 1))
+
+        @pl.when(b != 0)
+        def _():
+            greet((t, NB * lax.rem(a + 1, NA)))
+
+        greet((t, NB * a + lax.rem(b + 2, NB)))
+
+        @pl.when(half == 1)
+        def _():
+            greet((t, NB * a + lax.rem(b + 1, NB)))
+            greet((t, NB * a + lax.rem(b + 3, NB)))
+
+        for i in (2, 1, 3, 0):
+            for k in range(2):
+                greet(owner_device(lax.rem(b + i, NB), k))
+        greet((t + 1 - 2 * half, p))
+        pl.semaphore_wait(barrier, (NA - 1) + 1 + 8 + 1 + jnp.where(on_side, 1, 0))
 
     @pl.when(is_owner)
     def _():
-        pltpu.make_async_copy(kap_ref.at[layer_own], Ki.at[0], rI.at[0]).start()
-        pltpu.make_async_copy(src_ref.at[layer_own], Ki.at[1], rI.at[1]).start()
-        pltpu.make_async_copy(init_ref.at[layer_own], Ki.at[2], rI.at[2]).start()
-
-    pl.semaphore_wait(barrier, (SLICES * NB - 1) + (NA - 1) + 2 * (NB - 1))
+        def greet_slices(i, c):
+            for h in range(NC):
+                greet(fine_device(lax.rem(2 * b + 4 + i, SLICES), h))
+            return c
+
+        lax.fori_loop(0, SLICES, greet_slices, 0)
+        greet(owner_device(b, 1 - pair))
+        pltpu.make_async_copy(kap_ref.at[owned], Ki.at[0], rI.at[0]).start()
+        pltpu.make_async_copy(src_ref.at[owned], Ki.at[1], rI.at[1]).start()
+        pltpu.make_async_copy(init_ref.at[owned], Ki.at[2], rI.at[2]).start()
+        pl.semaphore_wait(barrier, 16 + 3 + jnp.where(on_side, 2, 0))
+
+    @pl.when(is_helper)
+    def _():
+        for k in range(2):
+            greet(owner_device(b, k))
+        pl.semaphore_wait(barrier, 2 + jnp.where(on_side, 2, 0))
 
     first = pl.multiple_of(half * BY, 8)
     window = pl.ds(pl.multiple_of(half * (NY - WIN), 8), WIN)
@@ -262,21 +287,21 @@
     def give(it, n):
         for h in range(NC):
             send(
-                UB.at[it, n, pl.ds(BY * h, BY), :],
-                ST.at[it, pl.ds(pl.multiple_of(BY * (SLAB * b + layer_own), BY), BY), :],
+                UB.at[it, n, :, pl.ds(BY * h, BY), :],
+                ST.at[it, pl.ds(SLAB * b + 2 * pair, 2)],
                 sS.at[it], rS.at[it], fine_device(n, h),
             )
 
     def coarse(values):
-        Tc[:, 0:NY] = values.T
+        Tc[...] = values.reshape(2 * NY, NX).T
         rows = [Tc[pl.ds(i, 8, stride=16), :] for i in range(16)]
         for i, row in enumerate(local_apply(rows, CXc, WXc)):
             Tc[pl.ds(i, 8, stride=16), :] = row
-        Lc[...] = Tc[:, 0:NY].T
-        rows = [Lc[pl.ds(i, 8, stride=8), :] for i in range(8)]
+        Lc[...] = Tc[...].T
+        rows = [Lc[pl.ds(i, 16, stride=8), :] for i in range(8)]
         for i, row in enumerate(local_apply(rows, CYc, WYc)):
-            Lc[pl.ds(i, 8, stride=8), :] = row
-        return Lc[...]
+            Lc[pl.ds(i, 16, stride=8), :] = row
+        return Lc[...].reshape(2, NY, NX)
 
     @pl.when(is_owner)
     def _():
@@ -287,13 +312,11 @@
         UB[1, 0] = Ki[2]
         UB[2, 0] = Ki[2]
         give(0, 0)
-        Tc[...] = jnp.ones_like(Tc)
-        Tc[:, 0:NY] = Ki[0].T
+        Lc[...] = Ki[0].reshape(2 * NY, NX)
+        Tc[...] = Lc[...].T
         local_setup([Tc[pl.ds(i, 8, stride=16), :] for i in range(16)], coarse_dt, CXc, WXc)
-        Lc[...] = Ki[0]
-        local_setup([Lc[pl.ds(i, 8, stride=8), :] for i in range(8)], coarse_dt, CYc, WYc)
-        heat = coarse_dt * Ki[1]
-        Hi[...] = heat
+        local_setup([Lc[pl.ds(i, 16, stride=8), :] for i in range(8)], coarse_dt, CYc, WYc)
+        Hi[...] = coarse_dt * Ki[1]
 
         def advance(n, c):
             UB[0, n] = coarse(UB[0, n - 1] + Hi[...])
@@ -336,21 +359,12 @@
             W[count - 1 + i - 1] = above[i]
         block_coefficients(faces, E[place], U[place], length, C)
 
-    def split_apply(load, store, C, W, ms, mr, ssem, rsem, st, place, count, length, order, device):
-        rows = [load(i) for i in range(length)]
-        up, down = block_edges(rows, C)
-        ms[st, 0] = up
-        ms[st, 1] = down
-        for i in order:
-            which = jnp.where(place + i < count, 0, 1)
-            send(ms.at[st, which], mr.at[st, count - 1 - i], ssem.at[st], rsem.at[st], device(i))
-        solved = block_inner(rows, C)
-        wait_bytes(mr.at[st], rsem.at[st])
-        got = [mr[st, i] for i in range(count - 1)]
-        low = tree_sum(W[i] * got[i] for i in range(count - 1))
-        high = tree_sum(W[count - 1 + i] * got[i] for i in range(count - 1))
-        for i in range(length):
-            store(i, solved[i] + C[2, i] * low + C[3, i] * high)
+    def join(got, W):
+        count = len(got)
+        return (
+            tree_sum(W[i] * got[i] for i in range(count)),
+            tree_sum(W[count + i] * got[i] for i in range(count)),
+        )
 
     @pl.when(is_fine)
     def _():
@@ -393,64 +407,83 @@
             T[pl.ds(BY * z, BY), :] = kappa_z(z)
         for tile in range(4):
             T[pl.ds(NX * tile, NX), :] = T[pl.ds(NX * tile, NX), :].T
-        local_setup([T[pl.ds(i, 32, stride=16), :] for i in range(16)], fine_dt, Cx, Wx)
-
+        for g in range(2):
+            local_setup(
+                [T[pl.ds(2 * NX * g + i, 16, stride=16), :] for i in range(16)],
+                fine_dt, Cx.at[g], Wx.at[g],
+            )
         wait_bytes(ty_r, r1.at[1])
         split_setup(Gy, ty_r, Ey, Ly, Uy, My, Cy, Wy, half, NC, BY)
-        wait_bytes(tz_r, r1.at[0])
-        split_setup(Gz, tz_r, Ez, Lz, Uz, Mz, Cz, Wz, a, NA, BZ)
         wait_bytes(Sb, r0.at[1])
         for z in range(BZ):
             Sb[z] = fine_dt * Sb[z]
 
-        def fine_step(it, s):
-            st = it * FINE + s
-            V = ST.at[it]
-            for tile in range(4):
-                start = V[pl.ds(NX * tile, NX), :] + Sb[4 * tile : 4 * tile + 4].reshape(NX, NX)
-                T[pl.ds(NX * tile, NX), :] = start.T
-            rows = [T[pl.ds(i, 32, stride=16), :] for i in range(16)]
-            for i, row in enumerate(local_apply(rows, Cx, Wx)):
-                T[pl.ds(i, 32, stride=16), :] = row
-            for tile in range(4):
-                V[pl.ds(NX * tile, NX), :] = T[pl.ds(NX * tile, NX), :].T
-
-            def store_y(i, value):
-                V[pl.ds(i, BZ, stride=BY), :] = value
-
-            split_apply(
-                lambda i: V[pl.ds(i, BZ, stride=BY), :], store_y,
-                Cy, Wy, my_s, my_r, sym, ry, st, half, NC, BY, (1,), lambda i: partner,
-            )
-
-            def store_z(i, value):
-                V[pl.ds(BY * i, BY), :] = value
-
-            split_apply(
-                lambda i: V[pl.ds(BY * i, BY), :], store_z,
-                Cz, Wz, mz_s, mz_r, szm, rz, st, a, NA, BZ, FAR_FIRST, at_z,
-            )
+        def solve_xy(it, st):
+            V = ST.at[it].reshape(BZ * BY, NX)
+            for g in range(2):
+                for tile in range(2 * g, 2 * g + 2):
+                    start = V[pl.ds(NX * tile, NX), :] + Sb[4 * tile : 4 * tile + 4].reshape(NX, NX)
+                    T[pl.ds(NX * tile, NX), :] = start.T
+                rows = [T[pl.ds(2 * NX * g + i, 16, stride=16), :] for i in range(16)]
+                for i, row in enumerate(local_apply(rows, Cx.at[g], Wx.at[g])):
+                    T[pl.ds(2 * NX * g + i, 16, stride=16), :] = row
+                for tile in range(2 * g, 2 * g + 2):
+                    V[pl.ds(NX * tile, NX), :] = T[pl.ds(NX * tile, NX), :].T
+                C = Cy.at[:, :, pl.ds(8 * g, 8), :]
+                rows = [V[pl.ds(8 * BY * g + i, 8, stride=BY), :] for i in range(BY)]
+                up, down = block_edges(rows, C)
+                my_s[st, g] = jnp.where(half == 0, up, down)
+                send(my_s.at[st, g], my_r.at[st, g], sym.at[st, g], ry.at[st, g], partner)
+            for g in range(2):
+                C = Cy.at[:, :, pl.ds(8 * g, 8), :]
+                rows = [V[pl.ds(8 * BY * g + i, 8, stride=BY), :] for i in range(BY)]
+                solved = block_inner(rows, C)
+                wait_bytes(my_r.at[st, g], ry.at[st, g])
+                got = my_r[st, g]
+                low, high = (Wy[0, 8 * g : 8 * g + 8] * got, Wy[1, 8 * g : 8 * g + 8] * got)
+                for i in range(BY):
+                    V[pl.ds(8 * BY * g + i, 8, stride=BY), :] = (
+                        solved[i] + C[2, i] * low + C[3, i] * high
+                    )
+
+        def solve_z(it, st):
+            V = ST.at[it].reshape(BZ * BY, NX)
+            rows = [V[pl.ds(BY * i, BY), :] for i in range(BZ)]
+            up, down = block_edges(rows, Cz)
+            mz_s[st, 0] = up
+            mz_s[st, 1] = down
+            for i in FAR_FIRST:
+                which = jnp.where(a + i < NA, 0, 1)
+                send(mz_s.at[st, which], mz_r.at[st, NA - 1 - i], szm.at[st], rz.at[st], at_z(i))
+            solved = block_inner(rows, Cz)
+            wait_bytes(mz_r.at[st], rz.at[st])
+            low, high = join([mz_r[st, i] for i in range(NA - 1)], Wz)
+            for i in range(BZ):
+                V[pl.ds(BY * i, BY), :] = solved[i] + Cz[2, i] * low + Cz[3, i] * high
 
         for it in range(ITERS):
             wait_bytes(ST.at[it], rS.at[it])
+            solve_xy(it, it * FINE)
+            if it == 0:
+                wait_bytes(tz_r, r1.at[0])
+                split_setup(Gz, tz_r, Ez, Lz, Uz, Mz, Cz, Wz, a, NA, BZ)
 
             def one_step(s, c):
-                fine_step(it, s)
+                solve_z(it, it * FINE + s)
+                solve_xy(it, it * FINE + s + 1)
                 return c
 
-            lax.fori_loop(0, FINE, one_step, 0)
-
-            def hand_in(i, c):
-                bb = lax.rem(b + 2 + i, NB)
-                for k in range(SLAB):
+            lax.fori_loop(0, FINE - 1, one_step, 0)
+            solve_z(it, it * FINE + FINE - 1)
+
+            for i in (2, 1, 3, 0):
+                bb = lax.rem(b + i, NB)
+                for k in range(2):
                     send(
-                        ST.at[it, pl.ds(pl.multiple_of(BY * (SLAB * bb + k), BY), BY), :],
-                        FB.at[it, section, pl.ds(first, BY), :],
+                        ST.at[it, pl.ds(SLAB * bb + 2 * k, 2)],
+                        FB.at[it, section, :, pl.ds(first, BY), :],
                         sF.at[it], rF.at[it, section], owner_device(bb, k),
                     )
-                return c
-
-            lax.fori_loop(0, NB, hand_in, 0)
 
     @pl.when(is_owner)
     def _():
@@ -463,7 +496,7 @@
                 UB[it + 1, n + 1] = UB[it, n + 1] + value
                 if last_turn:
                     src = UB.at[it + 1, n + 1]
-                    dst = out_ref.at[0, layer_own]
+                    dst = out_ref.at[0, owned]
 
                     @pl.when(n == t)
                     def _():
@@ -481,9 +514,7 @@
 
             if not last_turn:
                 give(it + 1, 0)
-            lax.fori_loop(0, SLICES, correct, jnp.zeros((NY, NX), jnp.float32))
-
-    wait_bytes(out_ref, rO)
+            lax.fori_loop(0, SLICES, correct, jnp.zeros((2, NY, NX), jnp.float32))
 
     @pl.when(is_fine)
     def _():
@@ -494,7 +525,8 @@
 
         def drain(st, c):
             wait_bytes(mz_r.at[st], szm.at[st])
-            wait_bytes(my_r.at[st], sym.at[st])
+            for g in range(2):
+                wait_bytes(my_r.at[st, g], sym.at[st, g])
             return c
 
         lax.fori_loop(0, STEPS, drain, 0)
@@ -505,13 +537,18 @@
     def _():
         wait_bytes(Kz, s0.at[2])
 
-    @pl.when(is_owner)
+    @pl.when(odd)
     def _():
         wait_bytes(Kb.at[pl.ds(0, 2 * SLAB)], s0.at[0])
         wait_bytes(Sb.at[pl.ds(0, 2 * SLAB)], s0.at[1])
+
+    @pl.when(is_owner)
+    def _():
         for it in range(ITERS):
-            wait_bytes(ST.at[it], sS.at[it])
+            wait_bytes(FB.at[it], sS.at[it])
         wait_bytes(FB.at[0, pl.ds(0, SLICES - 1)], sO)
+
+    wait_bytes(out_ref, rO)
 
 
 def vm(*shape):
@@ -533,13 +570,13 @@
             vm(NA + 1, *zl), vm(NA, *zl), vm(NA, *zl), vm(NA, *zl),
             vm(NC + 1, *yl), vm(NC, *yl), vm(NC, *yl), vm(NC, *yl),
             vm(4, BZ, *zl), vm(4, BY, *yl), vm(2 * (NA - 1), *zl), vm(2 * (NC - 1), *yl),
-            vm(4, 16, 32, NX), vm(14, 32, NX), vm(BZ * BY, NX),
-            vm(3, NY, NX), vm(NY, NX), vm(4, 16, 8, NX), vm(14, 8, NX),
-            vm(4, 8, 8, NX), vm(14, 8, NX), vm(NX, NX), vm(NY, NX),
-            vm(ITERS, BZ * BY, NX), vm(ITERS, SLICES, NY, NX), vm(ITERS + 1, SLICES + 1, NY, NX),
-            vm(STEPS, 2, *zl), vm(STEPS, NA - 1, *zl), vm(STEPS, 2, *yl), vm(STEPS, NC - 1, *yl),
+            vm(2, 4, 16, 16, NX), vm(2, 14, 16, NX), vm(BZ * BY, NX),
+            vm(3, 2, NY, NX), vm(2, NY, NX), vm(4, 16, 8, NX), vm(14, 8, NX),
+            vm(4, 8, 16, NX), vm(14, 16, NX), vm(NX, 2 * NY), vm(2 * NY, NX),
+            vm(ITERS, BZ, BY, NX), vm(ITERS, SLICES, 2, NY, NX), vm(ITERS + 1, SLICES + 1, 2, NY, NX),
+            vm(STEPS, 2, *zl), vm(STEPS, NA - 1, *zl), vm(STEPS, 2, 8, NX), vm(STEPS, 2, 8, NX),
             dma((4,)), dma((3,)), dma((2,)), dma((2,)),
-            dma((STEPS,)), dma((STEPS,)), dma((STEPS,)), dma((STEPS,)),
+            dma((STEPS,)), dma((STEPS,)), dma((STEPS, 2)), dma((STEPS, 2)),
             dma((ITERS, SLICES)), dma((ITERS,)), dma((ITERS,)), dma((ITERS,)), dma, dma, dma((3,)),
         ],
         compiler_params=pltpu.CompilerParams(

time: 113 us -> 108 us (0.956)
  Pallas kernels: 108 us -> 104 us
    pallas_call x1, Pallas kernels: 108 us -> 104 us  [per_device(): pl.pallas_call(kernel, out_shape=jax.ShapeDtypeStruct((1, SLAB, NY, NX),...]
where the time goes in v2:
time: 108 us
  Pallas kernels  104 us (96%)
  local copies, waits for them, and re-layouts  3.37 us (3%)
    pallas_call x1, Pallas kernels, per_device(): pl.pallas_call(kernel, out_shape=jax.ShapeDtypeStruct((1, SLAB, NY, NX),...  104 us
    unnamed x7, local copies, waits for them, and re-layouts  3.37 us

profile of v2, /device:TPU:25, one launch (start us, length us, event | category | flops | bytes accessed | tf_op | source)
XLA Modules:
  0.0 107.6 jit_solution(6786079103858200289)
XLA Ops:
  0.0 0.0 copy-start
  0.0 0.9 copy-done
  0.9 0.0 copy-start.1
  0.9 0.9 copy-done.1
  1.8 0.0 copy-start.2
  1.8 0.9 copy-done.2
  2.7 104.2 %parareal.1 = f32[1,4,64,128]{3,2,1,0:T(8,128)S(1)} custom-call(f32[4,64,128]{2,1,0:T(8,128)S(1)} %copy-done, f32[4,64,128]{2,1,0:T(8,128)S(1)} %copy-done.1, f32[4,64,128]{2,1,0:T(8,128)S(1)} %copy-done.2), custom_call_target="tpu_custom_call" | custom-call | tf_op jit(solution)/shard_map/parareal/pallas_call | solution.py:562
  106.9 0.7 copy.5
Async XLA Ops:
  0.0 0.9 copy-start
  0.9 0.9 copy-start.1
  1.8 0.9 copy-start.2

commit v3 on v2

--- a/solution.py
+++ b/solution.py
@@ -157,7 +157,7 @@
     Ez, Lz, Uz, Mz, Ey, Ly, Uy, My, Cz, Cy, Wz, Wy, Cx, Wx, T,
     Ki, Hi, CXc, WXc, CYc, WYc, Tc, Lc,
     ST, FB, UB, mz_s, mz_r, my_s, my_r,
-    r0, s0, r1, s1, rz, szm, ry, sym, rF, sF, rS, sS, rO, sO, rI,
+    r0, s0, r1, s1, rz, szm, ry, sym, rF, sF, rS, sS, rO, sO, rI, kap, src,
 ):
     t = lax.axis_index("tm")
     p = lax.axis_index("pencil")
@@ -195,6 +195,9 @@
 
     barrier = pltpu.get_barrier_semaphore()
 
+    pltpu.make_async_copy(kap_ref, kap, rI.at[3]).start()
+    pltpu.make_async_copy(src_ref, src, rI.at[4]).start()
+
     def greet(dev):
         pl.semaphore_signal(barrier, inc=1, device_id=dev, device_id_type=MESH)
 
@@ -246,6 +249,7 @@
             greet(owner_device(b, k))
         pl.semaphore_wait(barrier, 2 + jnp.where(on_side, 2, 0))
 
+    wait_bytes(kap, rI.at[3])
     first = pl.multiple_of(half * BY, 8)
     window = pl.ds(pl.multiple_of(half * (NY - WIN), 8), WIN)
     mine = pl.ds(SLAB * b, SLAB)
@@ -255,11 +259,11 @@
 
         @pl.when(target != b)
         def _():
-            send(kap_ref.at[:, window, :], Kb.at[mine], s0.at[0], r0.at[0], (t, NB * a + target))
+            send(kap.at[:, window, :], Kb.at[mine], s0.at[0], r0.at[0], (t, NB * a + target))
 
         @pl.when(target == b)
         def _():
-            pltpu.make_async_copy(kap_ref.at[:, window, :], Kb.at[mine], r0.at[0]).start()
+            pltpu.make_async_copy(kap.at[:, window, :], Kb.at[mine], r0.at[0]).start()
 
     for side, layer, da in ((NB - 1, SLAB - 1, 1), (0, 0, NA - 1)):
 
@@ -267,22 +271,23 @@
         def _():
             for i in range(2):
                 send(
-                    kap_ref.at[layer, pl.ds(first, BY), :],
+                    kap.at[layer, pl.ds(first, BY), :],
                     Kz.at[0 if da == 1 else 1],
                     s0.at[2], r0.at[2 if da == 1 else 3],
                     (t, NB * lax.rem(a + da, NA) + even + 2 * i),
                 )
 
+    wait_bytes(src, rI.at[4])
     for i in range(2):
         target = even + 2 * i
 
         @pl.when(target != b)
         def _():
-            send(src_ref.at[:, pl.ds(first, BY), :], Sb.at[mine], s0.at[1], r0.at[1], (t, NB * a + target))
+            send(src.at[:, pl.ds(first, BY), :], Sb.at[mine], s0.at[1], r0.at[1], (t, NB * a + target))
 
         @pl.when(target == b)
         def _():
-            pltpu.make_async_copy(src_ref.at[:, pl.ds(first, BY), :], Sb.at[mine], r0.at[1]).start()
+            pltpu.make_async_copy(src.at[:, pl.ds(first, BY), :], Sb.at[mine], r0.at[1]).start()
 
     def give(it, n):
         for h in range(NC):
@@ -446,15 +451,16 @@
                         solved[i] + C[2, i] * low + C[3, i] * high
                     )
 
+        ring = [(i, at_z(i), jnp.where(a + i < NA, 0, 1)) for i in FAR_FIRST]
+
         def solve_z(it, st):
             V = ST.at[it].reshape(BZ * BY, NX)
             rows = [V[pl.ds(BY * i, BY), :] for i in range(BZ)]
             up, down = block_edges(rows, Cz)
             mz_s[st, 0] = up
             mz_s[st, 1] = down
-            for i in FAR_FIRST:
-                which = jnp.where(a + i < NA, 0, 1)
-                send(mz_s.at[st, which], mz_r.at[st, NA - 1 - i], szm.at[st], rz.at[st], at_z(i))
+            for i, device, which in ring:
+                send(mz_s.at[st, which], mz_r.at[st, NA - 1 - i], szm.at[st], rz.at[st], device)
             solved = block_inner(rows, Cz)
             wait_bytes(mz_r.at[st], rz.at[st])
             low, high = join([mz_r[st, i] for i in range(NA - 1)], Wz)
@@ -495,16 +501,16 @@
                 value = coarse(before) + (FB[it, n] - UB[it, n + 1])
                 UB[it + 1, n + 1] = UB[it, n + 1] + value
                 if last_turn:
-                    src = UB.at[it + 1, n + 1]
+                    done = UB.at[it + 1, n + 1]
                     dst = out_ref.at[0, owned]
 
                     @pl.when(n == t)
                     def _():
-                        pltpu.make_async_copy(src, dst, rO).start()
+                        pltpu.make_async_copy(done, dst, rO).start()
 
                     @pl.when(n != t)
                     def _():
-                        send(src, dst, sO, rO, (n, p))
+                        send(done, dst, sO, rO, (n, p))
                 else:
 
                     @pl.when(n + 1 < SLICES)
@@ -577,10 +583,11 @@
             vm(STEPS, 2, *zl), vm(STEPS, NA - 1, *zl), vm(STEPS, 2, 8, NX), vm(STEPS, 2, 8, NX),
             dma((4,)), dma((3,)), dma((2,)), dma((2,)),
             dma((STEPS,)), dma((STEPS,)), dma((STEPS, 2)), dma((STEPS, 2)),
-            dma((ITERS, SLICES)), dma((ITERS,)), dma((ITERS,)), dma((ITERS,)), dma, dma, dma((3,)),
+            dma((ITERS, SLICES)), dma((ITERS,)), dma((ITERS,)), dma((ITERS,)), dma, dma, dma((5,)),
+            vm(SLAB, NY, NX), vm(SLAB, NY, NX),
         ],
         compiler_params=pltpu.CompilerParams(
-            collective_id=0, has_side_effects=True, vmem_limit_bytes=48 * 1024 * 1024
+            collective_id=0, has_side_effects=True, vmem_limit_bytes=60 * 1024 * 1024
         ),
         name="parareal",
     )(initial, conductivity, source)

time: 108 us -> 107 us (level)
  local copies, waits for them, and re-layouts: 3.37 us -> 1.57 us
    unnamed x7 -> x1, local copies, waits for them, and re-layouts: 3.37 us -> 1.57 us
where the time goes in v3:
time: 107 us
  Pallas kernels  105 us (98%)
  local copies, waits for them, and re-layouts  1.57 us (1%)
    pallas_call x1, Pallas kernels, per_device(): pl.pallas_call(kernel, out_shape=jax.ShapeDtypeStruct((1, SLAB, NY, NX),...  105 us

profile of v3, /device:TPU:25, one launch (start us, length us, event | category | flops | bytes accessed | tf_op | source)
XLA Modules:
  0.0 106.7 jit_solution(15403654459313707800)
XLA Ops:
  0.0 105.1 %parareal.1 = f32[1,4,64,128]{3,2,1,0:T(8,128)} custom-call(f32[4,64,128]{2,1,0:T(8,128)} %init_ref.1, f32[4,64,128]{2,1,0:T(8,128)} %kap_ref.1, f32[4,64,128]{2,1,0:T(8,128)} %src_ref.1), custom_call_target="tpu_custom_call" | custom-call | tf_op jit(solution)/shard_map/parareal/pallas_call | solution.py:568
  105.1 1.6 %copy.5 = f32[1,4,64,128]{3,2,1,0:T(8,128)} copy(f32[1,4,64,128]{3,2,1,0:T(8,128)} %parareal.1) | data formatting | bytes 262144

commit v4 on v3

--- a/solution.py
+++ b/solution.py
@@ -425,6 +425,7 @@
 
         def solve_xy(it, st):
             V = ST.at[it].reshape(BZ * BY, NX)
+            kept = []
             for g in range(2):
                 for tile in range(2 * g, 2 * g + 2):
                     start = V[pl.ds(NX * tile, NX), :] + Sb[4 * tile : 4 * tile + 4].reshape(NX, NX)
@@ -436,13 +437,13 @@
                     V[pl.ds(NX * tile, NX), :] = T[pl.ds(NX * tile, NX), :].T
                 C = Cy.at[:, :, pl.ds(8 * g, 8), :]
                 rows = [V[pl.ds(8 * BY * g + i, 8, stride=BY), :] for i in range(BY)]
+                kept.append(rows)
                 up, down = block_edges(rows, C)
                 my_s[st, g] = jnp.where(half == 0, up, down)
                 send(my_s.at[st, g], my_r.at[st, g], sym.at[st, g], ry.at[st, g], partner)
             for g in range(2):
                 C = Cy.at[:, :, pl.ds(8 * g, 8), :]
-                rows = [V[pl.ds(8 * BY * g + i, 8, stride=BY), :] for i in range(BY)]
-                solved = block_inner(rows, C)
+                solved = block_inner(kept[g], C)
                 wait_bytes(my_r.at[st, g], ry.at[st, g])
                 got = my_r[st, g]
                 low, high = (Wy[0, 8 * g : 8 * g + 8] * got, Wy[1, 8 * g : 8 * g + 8] * got)

time: 107 us -> 106 us (level)
  no operation moved by 1% of the time
where the time goes in v4:
time: 106 us
  Pallas kernels  104 us (98%)
  local copies, waits for them, and re-layouts  1.57 us (1%)
    pallas_call x1, Pallas kernels, per_device(): pl.pallas_call(kernel, out_shape=jax.ShapeDtypeStruct((1, SLAB, NY, NX),...  104 us

profile of v4, /device:TPU:25, one launch (start us, length us, event | category | flops | bytes accessed | tf_op | source)
XLA Modules:
  0.0 105.7 jit_solution(6872388213688488385)
XLA Ops:
  0.0 104.1 %parareal.1 = f32[1,4,64,128]{3,2,1,0:T(8,128)} custom-call(f32[4,64,128]{2,1,0:T(8,128)} %init_ref.1, f32[4,64,128]{2,1,0:T(8,128)} %kap_ref.1, f32[4,64,128]{2,1,0:T(8,128)} %src_ref.1), custom_call_target="tpu_custom_call" | custom-call | tf_op jit(solution)/shard_map/parareal/pallas_call | solution.py:569
  104.2 1.6 %copy.5 = f32[1,4,64,128]{3,2,1,0:T(8,128)} copy(f32[1,4,64,128]{3,2,1,0:T(8,128)} %parareal.1) | data formatting | bytes 262144

commit v5 on v4

--- a/solution.py
+++ b/solution.py
@@ -251,20 +251,27 @@
 
     wait_bytes(kap, rI.at[3])
     first = pl.multiple_of(half * BY, 8)
-    window = pl.ds(pl.multiple_of(half * (NY - WIN), 8), WIN)
+    inside = pl.ds(pl.multiple_of(8 * half, 8), BY)
+    beside = pl.ds(pl.multiple_of(BY - BY * half, 8), 8)
+    beside_src = pl.ds(pl.multiple_of(BY - 8 * half, 8), 8)
     mine = pl.ds(SLAB * b, SLAB)
     even = lax.rem(y, 2)
-    for i in range(2):
-        target = even + 2 * i
-
-        @pl.when(target != b)
-        def _():
-            send(kap.at[:, window, :], Kb.at[mine], s0.at[0], r0.at[0], (t, NB * a + target))
-
-        @pl.when(target == b)
-        def _():
-            pltpu.make_async_copy(kap.at[:, window, :], Kb.at[mine], r0.at[0]).start()
-
+
+    def spread(src_rows, dst_rows, ssem, rsem):
+        for i in range(2):
+            target = even + 2 * i
+            here = kap.at[:, src_rows, :]
+            there = Kb.at[mine, dst_rows, :]
+
+            @pl.when(target != b)
+            def _():
+                send(here, there, ssem, rsem, (t, NB * a + target))
+
+            @pl.when(target == b)
+            def _():
+                pltpu.make_async_copy(here, there, rsem).start()
+
+    spread(pl.ds(first, BY), inside, s0.at[0], r0.at[0])
     for side, layer, da in ((NB - 1, SLAB - 1, 1), (0, 0, NA - 1)):
 
         @pl.when(b == side)
@@ -277,6 +284,7 @@
                     (t, NB * lax.rem(a + da, NA) + even + 2 * i),
                 )
 
+    spread(beside_src, beside, s0.at[3], r0.at[4])
     wait_bytes(src, rI.at[4])
     for i in range(2):
         target = even + 2 * i
@@ -373,7 +381,7 @@
 
     @pl.when(is_fine)
     def _():
-        wait_bytes(Kb, r0.at[0])
+        wait_bytes(Kb.at[:, inside, :], r0.at[0])
         wait_bytes(Kz.at[0], r0.at[2])
         wait_bytes(Kz.at[1], r0.at[3])
         row0 = 8 * half
@@ -403,6 +411,7 @@
         for i in FAR_FIRST:
             send(tz_s, tz_r.at[a], s1.at[0], r1.at[0], at_z(i))
         pltpu.make_async_copy(tz_s, tz_r.at[a], r1.at[0]).start()
+        wait_bytes(Kb.at[:, beside, :], r0.at[4])
         outside(Gy, ty_s, kappa_y(-1), kappa_y, kappa_y(BY), half == 0, half == 1, fine_dt, BY)
         partner = (t + 1 - 2 * half, p)
         send(ty_s, ty_r.at[half], s1.at[1], r1.at[1], partner)
@@ -525,7 +534,8 @@
 
     @pl.when(is_fine)
     def _():
-        wait_bytes(Kb.at[pl.ds(0, SLAB)], s0.at[0])
+        wait_bytes(Kb.at[pl.ds(0, SLAB), inside, :], s0.at[0])
+        wait_bytes(Kb.at[pl.ds(0, SLAB), beside, :], s0.at[3])
         wait_bytes(Sb.at[pl.ds(0, SLAB)], s0.at[1])
         wait_bytes(tz_r.at[pl.ds(0, NA - 1)], s1.at[0])
         wait_bytes(ty_s, s1.at[1])
@@ -546,7 +556,8 @@
 
     @pl.when(odd)
     def _():
-        wait_bytes(Kb.at[pl.ds(0, 2 * SLAB)], s0.at[0])
+        wait_bytes(Kb.at[pl.ds(0, 2 * SLAB), inside, :], s0.at[0])
+        wait_bytes(Kb.at[pl.ds(0, 2 * SLAB), beside, :], s0.at[3])
         wait_bytes(Sb.at[pl.ds(0, 2 * SLAB)], s0.at[1])
 
     @pl.when(is_owner)
@@ -582,7 +593,7 @@
             vm(4, 8, 16, NX), vm(14, 16, NX), vm(NX, 2 * NY), vm(2 * NY, NX),
             vm(ITERS, BZ, BY, NX), vm(ITERS, SLICES, 2, NY, NX), vm(ITERS + 1, SLICES + 1, 2, NY, NX),
             vm(STEPS, 2, *zl), vm(STEPS, NA - 1, *zl), vm(STEPS, 2, 8, NX), vm(STEPS, 2, 8, NX),
-            dma((4,)), dma((3,)), dma((2,)), dma((2,)),
+            dma((5,)), dma((4,)), dma((2,)), dma((2,)),
             dma((STEPS,)), dma((STEPS,)), dma((STEPS, 2)), dma((STEPS, 2)),
             dma((ITERS, SLICES)), dma((ITERS,)), dma((ITERS,)), dma((ITERS,)), dma, dma, dma((5,)),
             vm(SLAB, NY, NX), vm(SLAB, NY, NX),

time: 106 us -> 106 us (level)
  no operation moved by 1% of the time
where the time goes in v5:
time: 106 us; the launch traced here: 105 us
  Pallas kernels  104 us (98%)
  local copies, waits for them, and re-layouts  1.57 us (1%)
    pallas_call x1, Pallas kernels, per_device(): pl.pallas_call(kernel, out_shape=jax.ShapeDtypeStruct((1, SLAB, NY, NX),...  104 us

profile of v5, /device:TPU:25, one launch (start us, length us, event | category | flops | bytes accessed | tf_op | source)
XLA Modules:
  0.0 105.1 jit_solution(16444146066745349920)
XLA Ops:
  0.0 103.5 %parareal.1 = f32[1,4,64,128]{3,2,1,0:T(8,128)} custom-call(f32[4,64,128]{2,1,0:T(8,128)} %init_ref.1, f32[4,64,128]{2,1,0:T(8,128)} %kap_ref.1, f32[4,64,128]{2,1,0:T(8,128)} %src_ref.1), custom_call_target="tpu_custom_call" | custom-call | tf_op jit(solution)/shard_map/parareal/pallas_call | solution.py:580
  103.6 1.6 %copy.5 = f32[1,4,64,128]{3,2,1,0:T(8,128)} copy(f32[1,4,64,128]{3,2,1,0:T(8,128)} %parareal.1) | data formatting | bytes 262144
